TPU v7x, 128 devices: a whole 4x4x4 slice. The times are simulated.
128 devices in a mesh: oct: 8 (over x, core), leaf: 16 (over y, z).
Axes of the slice: x: 4, y: 4, z: 4, core: 2. Of those that a mesh axis runs over, the one named last changes fastest.
Arguments:
- positions: bfloat16 [1024, 3, 512], P(('oct', 'leaf')), may hold values from 0.019897461 to 0.9765625
- charges: bfloat16 [1024, 32, 512], P(('oct', 'leaf')), may hold values from -6 to 6
- counts: int32 [1024], P(('oct', 'leaf')), may hold values from 32 to 512, as said below
- check_to_equiv: bfloat16 [64, 64], replicated, may hold values from -1.5 to 1.5
- up_child: bfloat16 [8, 64, 64], replicated, may hold values from -0.25 to 0.25
- down_child: bfloat16 [8, 64, 64], replicated, may hold values from -0.75 to 0.75
- translate: bfloat16 [343, 64, 64], replicated, may hold values from -0.0546875 to 0.0546875
Outputs:
- potential: float32 [1024, 32, 512], P(('oct', 'leaf'))
Inputs may be any that keep to these rules, and one draw needn't show every extreme that they name: Leaf m's live points are slots 0 to counts[m] - 1; in every draw all 8 leaves of one aligned block of 8 leaves are full.
All inputs are finite; a program needn't handle non-finite values.
Results may differ from a plain program's by a relative error of at most 0.00055.
The roundings to bfloat16 on the way count: a program that leaves them out, or rounds other values in their place, can miss the bound.
Values may be sent and summed in bfloat16 or wider, within the bound.
No kernel may reach another device: no remote copies, remote signals or barrier semaphores. Data moves between devices by JAX's collectives and lax.ppermute only.
A program may use at most 192 MiB of HBM per device.

v0:
```python
import functools

import jax
import jax.numpy as jnp
import numpy as np
from jax import lax
from jax.experimental import pallas as pl
from jax.experimental.pallas import tpu as pltpu
from jax.sharding import PartitionSpec as P

AXES = ("oct", "leaf")
KERNEL_SCALE = 0.02
SOFTENING = 0.01
INVERSE = 1.0 / KERNEL_SCALE**2
CHUNK = 128
ROWS = 144
FEATURES = 48
MIB = 1 << 20
F32 = jnp.float32
BF16 = jnp.bfloat16
VMEM = pl.BlockSpec(memory_space=pltpu.VMEM)
SMEM = pl.BlockSpec(memory_space=pltpu.SMEM)


def bit_counts(total):
    return [(total + 2) // 3, (total + 1) // 3, total // 3]


def box_coords(index, total):
    coords = []
    for j, bits in enumerate(bit_counts(total)):
        value = 0
        for k in range(bits):
            value = value + ((index >> (3 * k + j)) & 1) * 2**k
        coords.append(value)
    return coords


def box_index(coords, total):
    index = 0
    for j, bits in enumerate(bit_counts(total)):
        for k in range(bits):
            index = index + ((coords[j] >> k) & 1) * 2 ** (3 * k + j)
    return index


def shifted(value, axis, step, total):
    pairs = []
    for device in range(2**total):
        coords = box_coords(device, total)
        coords[axis] += step
        if 0 <= coords[axis] < 2 ** bit_counts(total)[axis]:
            pairs.append((device, box_index(coords, total)))
    return lax.ppermute(value, AXES, pairs)


def pieces(x):
    first = x.astype(BF16).astype(F32)
    rest = x - first
    second = rest.astype(BF16).astype(F32)
    third = (rest - second).astype(BF16).astype(F32)
    return first, second, third


def row_index(shape):
    return lax.broadcasted_iota(jnp.int32, shape, 0)


def placed(rows, offsets):
    eight = jnp.concatenate([rows, jnp.zeros_like(rows)], 0)
    index = row_index(eight.shape)
    shift = jnp.where(index == 0, offsets[0], jnp.where(index == 1, offsets[1], offsets[2]))
    return jnp.where(index < 3, eight + shift, 0.0)


def with_rows(base, extra):
    index = row_index(base.shape)
    for k, row in enumerate(extra):
        base = jnp.where(index == 3 + k, row, base)
    return base


def source_features(rows, offsets):
    x = placed(rows, offsets)
    high = x.astype(BF16).astype(F32)
    low = x - high
    norm = INVERSE * jnp.sum(x * x, axis=0, keepdims=True)
    ones = (1.0, 1.0, 1.0)
    groups = [with_rows(high, pieces(norm)), with_rows(high, ones), high, low, low, low]
    return jnp.concatenate(groups, 0)


def target_features(rows, offsets):
    x = placed(rows, offsets)
    w1, w2, w3 = pieces((-2.0 * INVERSE) * x)
    norm = INVERSE * (jnp.sum(x * x, axis=0, keepdims=True) + SOFTENING)
    ones = (1.0, 1.0, 1.0)
    return jnp.concatenate(
        [with_rows(w1, ones), with_rows(w2, pieces(norm)), w3, w1, w2, w3], 0
    )


def upward_kernel(counts, positions, charges, to_equiv, low, high, shape_out, equiv_out):
    n_points = positions.shape[2]
    n_chunks = n_points // CHUNK
    index = lax.broadcasted_iota(jnp.int32, (64, n_points), 0)
    surface = [
        ((index >> (2 * d)) & 3).astype(F32) * 0.5 - 0.25 for d in range(3)
    ]
    slot = lax.broadcasted_iota(jnp.int32, (32, n_points), 1)
    points = [positions[d].astype(F32) for d in range(3)]
    upward = []
    for leaf in range(8):
        out, at = (low, leaf) if leaf < 4 else (high, leaf - 4)
        count = counts[leaf]
        p = [points[d][leaf : leaf + 1] for d in range(3)]
        square = (surface[0] - p[0]) ** 2
        square = square + (surface[1] - p[1]) ** 2
        square = square + (surface[2] - p[2]) ** 2
        shape = (KERNEL_SCALE * lax.rsqrt(square + SOFTENING)).astype(BF16)
        shape_out[leaf] = shape
        q = jnp.where(slot < count, charges[leaf].astype(F32), 0.0).astype(BF16)
        upward.append(
            lax.dot_general(q, shape, (((1,), (1,)), ((), ())), preferred_element_type=F32)
        )
        live = lax.shift_right_logical(count + (CHUNK - 1), 7).astype(F32)
        rows = []
        for j in range(n_chunks):
            at_lanes = slice(CHUNK * j, CHUNK * (j + 1))
            out[at, 32 * j : 32 * j + 32, :] = q[:, at_lanes]
            rows += [row[:, at_lanes] for row in p]
            rows.append(jnp.full((1, CHUNK), live, F32))
        out[at, 128:144, :] = jnp.concatenate(rows, 0).astype(BF16)
    total = jnp.concatenate(upward, 0)
    equiv = jnp.zeros(total.shape, F32)
    for piece in pieces(total)[::-1]:
        equiv = equiv + jnp.dot(piece.astype(BF16), to_equiv[...], preferred_element_type=F32)
    equiv = equiv.astype(BF16)
    equiv_out[...] = jnp.concatenate([equiv[32 * l : 32 * l + 32] for l in range(8)], 1)


def targets_kernel(low, high, targets):
    for leaf in range(8):
        src, at = (low, leaf) if leaf < 4 else (high, leaf - 4)
        offsets = (leaf % 2 - 1.0, leaf // 2 % 2 - 1.0, leaf // 4 - 1.0)
        block = src[at, 128:144, :].astype(F32)
        for j in range(4):
            features = target_features(block[4 * j : 4 * j + 4], offsets)
            targets[4 * leaf + j] = features.T.astype(BF16)


def near_kernel(sides, with_before, leaves, sources, aims, *refs):
    payloads, refs = refs[: len(sides)], refs[len(sides) :]
    targets, refs = refs[0], refs[1:]
    if with_before:
        before, refs = refs[0], refs[1:]
    counts, out, features, values, live_v, live_s, queue, aim_queue, sem = refs
    n_leaves = sum(sides)
    n_tasks, n_sources = sources.shape
    n_aims = aims.shape[1]
    first = 0
    for payload, size in zip(payloads, sides):

        def one(leaf, _, payload=payload, first=first):
            block = payload[leaf, 128:144, :].astype(F32)
            at = first + leaf
            offsets = [leaves[at, d].astype(F32) for d in range(3)]
            for j in range(4):
                features[4 * at + j] = source_features(block[4 * j : 4 * j + 4], offsets).astype(
                    BF16
                )
                values[4 * at + j] = payload[leaf, 32 * j : 32 * j + 32, :]
            live_v[pl.ds(at, 1), :] = block[3:4].astype(jnp.int32)
            return 0

        lax.fori_loop(0, size, one, 0)
        first += size
    features[4 * n_leaves] = features[0]
    values[4 * n_leaves] = jnp.zeros((32, CHUNK), BF16)
    copy = pltpu.make_async_copy(live_v, live_s, sem)
    copy.start()
    copy.wait()
    out[...] = before[...] if with_before else jnp.zeros_like(out)

    def compute(start, n_rows, n_items):
        places = [aim_queue[start + i] for i in range(n_rows)]
        rows = jnp.concatenate([targets[place] for place in places], 0)

        def add(at, width, total):
            items = [queue[at + k] for k in range(width)]
            u = jnp.concatenate([features[item] for item in items], 1)
            q = jnp.concatenate([values[item] for item in items], 1)
            square = jnp.dot(rows, u, preferred_element_type=F32)
            kern = lax.rsqrt(square).astype(BF16)
            return total + lax.dot_general(
                q, kern, (((1,), (1,)), ((), ())), preferred_element_type=F32
            )

        def store(total):
            for i, place in enumerate(places):
                out[place] += total[:, CHUNK * i : CHUNK * (i + 1)]

        full = n_items // 12
        rest = n_items - 12 * full
        total = lax.fori_loop(
            0, full, lambda c, t: add(12 * c, 12, t), jnp.zeros((32, CHUNK * n_rows), F32)
        )
        store(total)
        for width in (4, 8, 12):

            @pl.when((rest > width - 4) & (rest <= width))
            def _(width=width):
                store(add(12 * full, width, jnp.zeros((32, CHUNK * n_rows), F32)))

    def task(i, _):
        n_items = jnp.int32(0)
        for k in range(n_sources):
            leaf = sources[i, k]
            n_live = jnp.where(leaf >= 0, live_s[jnp.maximum(leaf, 0), 0], 0)
            for j in range(4):
                queue[n_items] = 4 * leaf + j
                n_items = n_items + (j < n_live).astype(jnp.int32)
        for k in range(12):
            queue[n_items + k] = 4 * n_leaves
        n_rows = jnp.int32(0)
        for k in range(n_aims):
            leaf = aims[i, k]
            count = jnp.where(leaf >= 0, counts[jnp.maximum(leaf, 0)], 0)
            for j in range(4):
                aim_queue[n_rows] = 4 * leaf + j
                n_rows = n_rows + (CHUNK * j < count).astype(jnp.int32)

        @pl.when(n_items > 0)
        def _():
            full = n_rows // 4

            def four(c, _):
                compute(4 * c, 4, n_items)
                return 0

            lax.fori_loop(0, full, four, 0)
            for rest in (1, 2, 3):

                @pl.when(n_rows - 4 * full == rest)
                def _(rest=rest):
                    compute(4 * full, rest, n_items)

        return 0

    lax.fori_loop(0, n_tasks, task, 0)


def faces_kernel(x_low, z_low, low, high, z_high, x_high, *faces):
    for y in range(2):
        for z, plane in enumerate((z_low, low, high, z_high)):
            faces[y][4 * z] = x_low[2 * z + y]
            faces[y][4 * z + 1] = plane[2 * y]
            faces[y][4 * z + 2] = plane[2 * y + 1]
            faces[y][4 * z + 3] = x_high[2 * z + y]


def widen_kernel(table, wide, rows):
    n_equiv = table.shape[0]
    window = 6 * n_equiv
    n_offsets = table.shape[2]
    n_lanes = 3 * CHUNK
    stride = n_equiv + 1
    together = 8
    unit = row_index((CHUNK, CHUNK)) == lax.broadcasted_iota(jnp.int32, (CHUNK, CHUNK), 1)
    unit = jnp.where(unit, 1.0, 0.0).astype(BF16)

    def turn(i, _):
        parts = []
        for m in range(together):
            x = jnp.concatenate(
                [
                    table[together * i + m].astype(F32),
                    jnp.zeros((n_equiv, n_lanes - n_offsets), F32),
                ],
                1,
            )
            parts += [pltpu.roll(x, n_lanes - 1, 1), x]
        both = jnp.concatenate(parts, 0).astype(BF16)
        for c in range(n_lanes // CHUNK):
            turned = lax.dot_general(
                unit,
                both[:, CHUNK * c : CHUNK * (c + 1)],
                (((1,), (1,)), ((), ())),
                preferred_element_type=F32,
            )
            for m in range(together):
                at = pl.ds(CHUNK * c * stride + together * i + m, CHUNK, stride=stride)
                rows[at, :] = turned[:, CHUNK * m : CHUNK * (m + 1)]
        return 0

    lax.fori_loop(0, n_equiv // together, turn, 0)
    index = lax.broadcasted_iota(jnp.int32, (window, 2 * n_equiv), 0)
    lane = lax.broadcasted_iota(jnp.int32, (window, 2 * n_equiv), 1)
    first = jnp.where(lane < n_equiv, n_equiv, 2 * n_equiv)
    beside = (index >= first) & (index < first + 3 * n_equiv)

    def pack(i, _):
        oz, oy = i // 7, i % 7
        near = (jnp.abs(oz - 3) <= 1) & (jnp.abs(oy - 3) <= 1)
        block = jnp.concatenate(
            [rows[pl.ds((7 * i + x) * stride, n_equiv), :] for x in range(6)], 0
        )
        block = jnp.where(near & beside, 0.0, block)
        wide[oz, pl.ds(pl.multiple_of(oy * window, window), window), :] = block.astype(BF16)
        return 0

    lax.fori_loop(0, 49, pack, 0)


def far_kernel(
    total_bits,
    counts,
    gathered_hbm,
    wide_hbm,
    up,
    down,
    shape,
    near,
    out,
    gathered,
    wide,
    boxes,
    region,
    sems,
):
    n_equiv = 64
    window = 6 * n_equiv
    bits = bit_counts(total_bits)
    n_pairs = gathered.shape[0]
    step = n_pairs // 4
    copies = []
    for i in range(4):
        part = pl.ds(step * i, step)
        copies.append(pltpu.make_async_copy(gathered_hbm.at[part], gathered.at[part], sems.at[i]))
    copies.append(pltpu.make_async_copy(wide_hbm, wide, sems.at[4]))
    for copy in copies:
        copy.start()
    me = lax.axis_index("oct") * lax.axis_size("leaf") + lax.axis_index("leaf")
    cx, cy, cz = box_coords(me, total_bits)
    zeros_up = jnp.zeros((8 * n_equiv, n_equiv), F32)
    up_rows = up[...].astype(F32).reshape(8 * n_equiv, n_equiv)
    up_even = jnp.concatenate([up_rows, zeros_up], 1).astype(BF16)
    up_odd = jnp.concatenate([zeros_up, up_rows], 1).astype(BF16)
    for i in range(4):
        copies[i].wait()
        at = slice(step * i, step * (i + 1))
        even = gathered[at, 0].reshape(step * 32, 8 * n_equiv)
        odd = gathered[at, 1].reshape(step * 32, 8 * n_equiv)
        both = jnp.dot(even, up_even, preferred_element_type=F32)
        both = both + jnp.dot(odd, up_odd, preferred_element_type=F32)
        boxes[at] = both.astype(BF16).reshape(step, 32, 2 * n_equiv)

    region[0] = jnp.zeros_like(region[0])
    region[7] = jnp.zeros_like(region[7])
    for bz in range(3):
        for by in range(3):
            for bx in range(3):
                z, y, x = cz + bz - 1, cy + by - 1, cx + bx - 1
                inside = (
                    (z >= 0)
                    & (z < 2 ** bits[2])
                    & (y >= 0)
                    & (y < 2 ** bits[1])
                    & (x >= 0)
                    & (x < 2 ** bits[0])
                )
                box = jnp.where(inside, box_index([x, y, z], total_bits), 0)
                data = gathered[box >> 1, box & 1]
                data = jnp.where(inside, data, jnp.zeros_like(data))
                for lz in range(2):
                    for ly in range(2):
                        at = (2 * by + ly) * window + bx * 2 * n_equiv
                        part = (2 * lz + ly) * 2 * n_equiv
                        region[1 + 2 * bz + lz, :, at : at + 2 * n_equiv] = data[
                            :, part : part + 2 * n_equiv
                        ]

    copies[4].wait()

    parent = cx >> 1
    total = jnp.zeros((32, 2 * n_equiv), F32)
    zero = jnp.zeros((32, 2 * n_equiv), BF16)
    span_y = 2 ** bits[1]
    for z in range(2 ** bits[2]):
        row = []
        for y in range(span_y):
            for dx in (-1, 0, 1):
                px = parent + dx
                inside = (px >= 0) & (px < 2 ** (bits[0] - 1))
                pair = box_index([2 * jnp.where(inside, px, 0), y, z], total_bits) >> 1
                row.append(jnp.where(inside, boxes[pair], zero))
        start = pl.multiple_of((3 - cy) * window, window)
        right = wide[z - cz + 3, pl.ds(start, span_y * window), :]
        total = total + jnp.dot(jnp.concatenate(row, 1), right, preferred_element_type=F32)
    total = jnp.where((cx & 1) == 0, total, pltpu.roll(total, n_equiv, 1))
    box_local = (0.5 * total[:, :n_equiv]).astype(BF16)
    down_row = jnp.concatenate([down[l] for l in range(8)], 1)
    inherited = jnp.dot(box_local, down_row, preferred_element_type=F32)

    sums = [jnp.zeros((64, 2 * n_equiv), F32) for _ in range(2)]
    for a in range(7):
        left = region[a : a + 2].reshape(64, 6 * window)
        for ty in range(2):
            right = wide[a, (1 - ty) * window : (7 - ty) * window, :]
            sums[ty] = sums[ty] + jnp.dot(left, right, preferred_element_type=F32)
    n_points = out.shape[2]
    slot = lax.broadcasted_iota(jnp.int32, (32, n_points), 1)
    lane = lax.broadcasted_iota(jnp.int32, (32, 2 * n_equiv), 1)
    for tz in range(2):
        for ty in range(2):
            first = 4 * tz + 2 * ty
            local = (
                inherited[:, first * n_equiv : (first + 2) * n_equiv]
                + sums[ty][32 * tz : 32 * tz + 32]
            )
            left = jnp.concatenate(
                [jnp.where(lane < n_equiv, local, 0.0), jnp.where(lane < n_equiv, 0.0, local)], 0
            ).astype(BF16)
            right = shape[first : first + 2].reshape(2 * n_equiv, n_points)
            far = jnp.dot(left, right, preferred_element_type=F32)
            for tx in range(2):
                value = jnp.concatenate([near[4 * (first + tx) + j] for j in range(4)], 1)
                value = value + far[32 * tx : 32 * tx + 32]
                out[first + tx] = jnp.where(slot < counts[first + tx], value, 0.0)


def call(kernel, ins, outs, scratch=(), flops=0, seen=0, limit=28, **kwargs):
    return pl.pallas_call(
        kernel,
        out_shape=outs,
        in_specs=ins,
        out_specs=jax.tree.map(lambda _: VMEM, outs),
        scratch_shapes=list(scratch),
        compiler_params=pltpu.CompilerParams(vmem_limit_bytes=limit * MIB),
        cost_estimate=pl.CostEstimate(flops=flops, bytes_accessed=seen, transcendentals=0),
        **kwargs,
    )


def near_tables():
    both = range(2)
    own = [(x, y, z) for z in (1, 2) for y in (1, 2) for x in (1, 2)]
    z_side = [(x, y, 3 * side) for side in both for y in (1, 2) for x in (1, 2)]
    x_side = [(3 * side, y, z) for side in both for z in range(4) for y in (1, 2)]
    y_side = [(x, 3 * side, z) for side in both for z in range(4) for x in range(4)]
    eight = list(range(8))
    middle = []
    for side in both:
        four = [4 * side + i for i in range(4)]
        middle.append((four, four))
    for tx in both:
        for tz in both:
            six = [8 + 8 * tx + 2 * tz + i for i in range(6)]
            middle.append((six, [4 * tz + 2 * ty + tx for ty in both]))
    last = []
    for ty in both:
        for tz in both:
            for tx in both:
                nine = [
                    16 * ty + 4 * (tz + dz) + tx + dx for dz in range(3) for dx in range(3)
                ]
                last.append((nine, [4 * tz + 2 * ty + tx]))
    return {
        "first": ((4, 4), own, [(eight, [0, 1, 2, 3])]),
        "second": ((4, 4), own, [(eight, [4, 5, 6, 7])]),
        "middle": ((4, 4, 8, 8), z_side + x_side, middle),
        "last": ((16, 16), y_side, last),
    }


def near_call(phase, payloads, targets, counts, before):
    sides, places, tasks = near_tables()[phase]
    n_leaves = sum(sides)
    n_sources = max(len(task[0]) for task in tasks)
    n_aims = max(len(task[1]) for task in tasks)
    pad = lambda row, size: row + [-1] * (size - len(row))
    tables = [
        np.array(places, np.int32) - 2,
        np.array([pad(task[0], n_sources) for task in tasks], np.int32),
        np.array([pad(task[1], n_aims) for task in tasks], np.int32),
    ]
    args = [jnp.asarray(table) for table in tables] + list(payloads) + [targets]
    if before is not None:
        args.append(before)
    args.append(counts)
    us = {"first": 12, "second": 12, "middle": 25, "last": 15}[phase]
    return call(
        functools.partial(near_kernel, sides, before is not None),
        [SMEM] * 3 + [VMEM] * (len(args) - 4) + [SMEM],
        jax.ShapeDtypeStruct((32, 32, CHUNK), F32),
        [
            pltpu.VMEM((4 * n_leaves + 1, FEATURES, CHUNK), BF16),
            pltpu.VMEM((4 * n_leaves + 1, 32, CHUNK), BF16),
            pltpu.VMEM((n_leaves, CHUNK), jnp.int32),
            pltpu.SMEM((n_leaves, CHUNK), jnp.int32),
            pltpu.SMEM((64,), jnp.int32),
            pltpu.SMEM((40,), jnp.int32),
            pltpu.SemaphoreType.DMA,
        ],
        flops=us * 10**9,
        seen=us * 10**6,
        name="near_" + phase,
    )(*args)


def per_device(positions, charges, counts, check_to_equiv, up_child, down_child, translate):
    n_points = positions.shape[2]
    n_probe = charges.shape[1]
    n_devices = lax.axis_size(AXES)
    total_bits = n_devices.bit_length() - 1
    shape_of = jax.ShapeDtypeStruct
    half = shape_of((4, ROWS, CHUNK), BF16)
    low, high, shape, equiv = call(
        upward_kernel,
        [SMEM, VMEM, VMEM, VMEM],
        (half, half, shape_of((8, 64, n_points), BF16), shape_of((n_probe, 512), BF16)),
        seen=3 * 10**6,
        flops=3 * 10**9,
        limit=56,
        name="upward",
    )(counts, positions.transpose(1, 0, 2), charges, check_to_equiv)
    move = functools.partial(shifted, total=total_bits)
    z_low = move(high, 2, 1)
    z_high = move(low, 2, -1)
    gathered = lax.all_gather(equiv, AXES, axis=0)
    targets = call(
        targets_kernel,
        [VMEM] * 2,
        shape_of((32, CHUNK, FEATURES), BF16),
        seen=10**6,
        flops=10**9,
        name="targets",
    )(low, high)
    near = near_call("first", (low, high), targets, counts, None)
    z_low, z_high, near = lax.optimization_barrier((z_low, z_high, near))
    planes = [a.reshape(2, 2, ROWS, CHUNK) for a in (z_low, low, high, z_high)]
    faces = [jnp.stack([a[:, x] for a in planes]).reshape(8, ROWS, CHUNK) for x in range(2)]
    faces[0], faces[1], near = lax.optimization_barrier((faces[0], faces[1], near))
    x_low = move(faces[1], 0, 1)
    x_high = move(faces[0], 0, -1)
    near = near_call("second", (low, high), targets, counts, near)
    x_low, x_high, near = lax.optimization_barrier((x_low, x_high, near))
    plane = shape_of((16, ROWS, CHUNK), BF16)
    y_faces = call(
        faces_kernel, [VMEM] * 6, (plane, plane), seen=3 * 10**6, flops=10**9, name="faces"
    )(x_low, z_low, low, high, z_high, x_high)
    face_0, face_1, near = lax.optimization_barrier((*y_faces, near))
    y_low = move(face_1, 1, 1)
    y_high = move(face_0, 1, -1)
    near = near_call("middle", (z_low, z_high, x_low, x_high), targets, counts, near)
    translate, near = lax.optimization_barrier((translate, near))
    wide = call(
        widen_kernel,
        [VMEM],
        shape_of((7, 7 * 6 * 64, 128), BF16),
        [pltpu.VMEM((3 * CHUNK * 65, 128), F32)],
        limit=56,
        seen=6 * 10**6,
        flops=6 * 10**9,
        name="widen",
    )(translate.transpose(1, 2, 0))
    wide, near, y_low, y_high = lax.optimization_barrier((wide, near, y_low, y_high))
    near = near_call("last", (y_low, y_high), targets, counts, near)
    anywhere = pl.BlockSpec(memory_space=pl.ANY)
    return call(
        functools.partial(far_kernel, total_bits),
        [SMEM, anywhere, anywhere] + [VMEM] * 4,
        shape_of((8, n_probe, n_points), F32),
        [
            pltpu.VMEM((n_devices // 2, 2, n_probe, 512), BF16),
            pltpu.VMEM((7, 7 * 6 * 64, 128), BF16),
            pltpu.VMEM((n_devices // 2, n_probe, 128), BF16),
            pltpu.VMEM((8, n_probe, 36 * 64), BF16),
            pltpu.SemaphoreType.DMA((5,)),
        ],
        seen=10 * 10**6,
        flops=8 * 10**9,
        limit=56,
        name="far",
    )(
        counts,
        gathered.reshape(n_devices // 2, 2, n_probe, 512),
        wide,
        up_child,
        down_child,
        shape,
        near,
    )


def solution(mesh):
    split = P(AXES, None, None)
    return jax.shard_map(
        per_device,
        mesh=mesh,
        in_specs=(split, split, P(AXES), P(), P(), P(), P()),
        out_specs=split,
        check_vma=False,
    )
```

profile of v0, /device:TPU:1, one launch (start us, length us, event | category | flops | bytes accessed | tf_op | source)
XLA Modules:
  0.0 113.7 jit_solution(7731339612319358297)
XLA Ops:
  6.6 2.5 %upward.1 = (bf16[4,144,128]{2,1,0:T(8,128)(2,1)}, bf16[4,144,128]{2,1,0:T(8,128)(2,1)}, bf16[8,64,512]{2,1,0:T(8,128)(2,1)}, bf16[32,512]{1,0:T(8,128)(2,1)}) custom-call(s32[8]{0:T(128)} %counts.3, bf16[3,8,512]{2,1,0:T(8,128)(2,1)} %bitcast.49, bf16[8,32,512]{2,1,0:T(8,128)(2,1)} %charges.1, bf16[64,64]{1,0:T(8,128)(2,1)} %to_equiv.1), custom_call_target="tpu_custom_call" | custom-call | flops 3000000000 | bytes 3000000 | tf_op jit(solution)/shard_map/upward/pallas_call | solution.py:518
  9.1 0.0 all-gather.3.cloned.1.call-update
  9.1 4.0 %collective-permute-start = (bf16[4,144,128]{2,1,0:T(8,128)(2,1)}, bf16[4,144,128]{2,1,0:T(8,128)(2,1)S(1)}, u32[]{:S(2)}, u32[]{:S(2)}) collective-permute-start(bf16[4,144,128]{2,1,0:T(8,128)(2,1)} %get-tuple-element.30.high.refs_1_), channel_id=1, source_target_pairs={{0,4},{1,5},{2,6},{3,7},{4,32},{5,33},{6,34},{7,35},{8,12},{9,13},... | collective-permute-start | bytes 442376 | tf_op jit(solution)/shard_map/ppermute | solution.py:54
  13.2 1.3 %collective-permute-start.1 = (bf16[4,144,128]{2,1,0:T(8,128)(2,1)}, bf16[4,144,128]{2,1,0:T(8,128)(2,1)S(1)}, u32[]{:S(2)}, u32[]{:S(2)}) collective-permute-start(bf16[4,144,128]{2,1,0:T(8,128)(2,1)} %get-tuple-element.31.low.refs_0_), channel_id=1, source_target_pairs={{4,0},{5,1},{6,2},{7,3},{12,8},{13,9},{14,10},{15,11},{20,16},{21,... | collective-permute-start | bytes 442376 | tf_op jit(solution)/shard_map/ppermute | solution.py:54
  14.5 0.0 copy-start
  14.5 0.9 copy-done
  15.4 0.9 copy-done.3
  16.3 0.4 targets.1.refs_2_.refs_4_
  16.7 0.9 copy-done.1
  17.6 0.9 copy-done.4
  18.6 3.3 %near_first.1.refs_3_ = f32[32,32,128]{2,1,0:T(8,128)S(1)} custom-call(s32[8,3]{1,0:T(8,128)S(1)} %copy-done.13, s32[1,8]{1,0:T(1,128)S(1)} %copy-done.14, s32[1,4]{1,0:T(1,128)S(1)} %copy-done.16, bf16[4,144,128]{2,1,0:T(8,128)(2,1)S(1)} %copy-done.1, bf16[4,144,128]{2,1,0:T(8,128)(2,1)S(1)} %copy-done.4, bf16[32,128,48]{2,1,0:T(8,128)(2,1)S(1)} %targets.1.refs_2_.refs_4_, ...), custom_call_target="tpu_custom_call" | custom-call | flops 12000000000 | bytes 12000000 | tf_op jit(solution)/shard_map/near_first/pallas_call | solution.py:492
  22.0 0.1 pad_maximum_fusion
  22.1 0.0 copy-start.8
  22.1 0.0 copy-start.11
  22.1 0.0 copy-start.12
  22.1 3.3 %collective-permute-start.2 = (bf16[8,144,128]{2,1,0:T(8,128)(2,1)S(1)}, bf16[8,144,128]{2,1,0:T(8,128)(2,1)S(1)}, u32[]{:S(2)}, u32[]{:S(2)}) collective-permute-start(bf16[8,144,128]{2,1,0:T(8,128)(2,1)S(1)} %bitcast.46), channel_id=1, source_target_pairs={{0,1},{1,8},{2,3},{3,10},{4,5},{5,12},{6,7},{7,14},{8,9},{9,64},{1... | collective-permute-start | bytes 884744 | tf_op jit(solution)/shard_map/ppermute | solution.py:54
  25.5 1.3 %collective-permute-start.3 = (bf16[8,144,128]{2,1,0:T(8,128)(2,1)S(1)}, bf16[8,144,128]{2,1,0:T(8,128)(2,1)S(1)}, u32[]{:S(2)}, u32[]{:S(2)}) collective-permute-start(bf16[8,144,128]{2,1,0:T(8,128)(2,1)S(1)} %bitcast.45), channel_id=1, source_target_pairs={{1,0},{3,2},{5,4},{7,6},{8,1},{9,8},{10,3},{11,10},{12,5},{13,12},... | collective-permute-start | bytes 884744 | tf_op jit(solution)/shard_map/ppermute | solution.py:54
  26.8 2.7 %near_second.1.refs_5_ = f32[32,32,128]{2,1,0:T(8,128)S(1)} custom-call(s32[8,3]{1,0:T(8,128)S(1)} %copy-done.13, s32[1,8]{1,0:T(1,128)S(1)} %copy-done.14, s32[1,4]{1,0:T(1,128)S(1)} %copy-done.15, bf16[4,144,128]{2,1,0:T(8,128)(2,1)S(1)} %copy-done.1, bf16[4,144,128]{2,1,0:T(8,128)(2,1)S(1)} %copy-done.4, bf16[32,128,48]{2,1,0:T(8,128)(2,1)S(1)} %targets.1.refs_2_.refs_4_, ...), custom_call_target="tpu_custom_call" | custom-call | flops 12000000000 | bytes 12000000 | tf_op jit(solution)/shard_map/near_second/pallas_call | solution.py:492
  29.5 6.4 %collective-permute-done.3.x_high.refs_3_ = bf16[8,144,128]{2,1,0:T(8,128)(2,1)S(1)} collective-permute-done((bf16[8,144,128]{2,1,0:T(8,128)(2,1)S(1)}, bf16[8,144,128]{2,1,0:T(8,128)(2,1)S(1)}, u32[]{:S(2)}, u32[]{:S(2)}) %collective-permute-start.3) | collective-permute-done | bytes 294944 | tf_op jit(solution)/shard_map/ppermute | solution.py:54
  35.9 0.1 faces.1
  36.0 9.3 %collective-permute-start.4 = (bf16[16,144,128]{2,1,0:T(8,128)(2,1)S(1)}, bf16[16,144,128]{2,1,0:T(8,128)(2,1)S(1)}, u32[]{:S(2)}, u32[]{:S(2)}) collective-permute-start(bf16[16,144,128]{2,1,0:T(8,128)(2,1)S(1)} %get-tuple-element.46), channel_id=1, source_target_pairs={{0,2},{1,3},{2,16},{3,17},{4,6},{5,7},{6,20},{7,21},{8,10},{9,11},... | collective-permute-start | bytes 1769480 | tf_op jit(solution)/shard_map/ppermute | solution.py:54
  45.4 2.1 %collective-permute-start.5 = (bf16[16,144,128]{2,1,0:T(8,128)(2,1)S(1)}, bf16[16,144,128]{2,1,0:T(8,128)(2,1)S(1)}, u32[]{:S(2)}, u32[]{:S(2)}) collective-permute-start(bf16[16,144,128]{2,1,0:T(8,128)(2,1)S(1)} %get-tuple-element.47), channel_id=1, source_target_pairs={{2,0},{3,1},{6,4},{7,5},{10,8},{11,9},{14,12},{15,13},{16,2},{17,3... | collective-permute-start | bytes 1769480 | tf_op jit(solution)/shard_map/ppermute | solution.py:54
  47.5 5.2 %near_middle.1.refs_3_ = f32[32,32,128]{2,1,0:T(8,128)S(1)} custom-call(s32[24,3]{1,0:T(8,128)S(1)} %copy-done.8, s32[6,6]{1,0:T(8,128)S(1)} %copy-done.11, s32[6,4]{1,0:T(8,128)S(1)} %copy-done.12, bf16[4,144,128]{2,1,0:T(8,128)(2,1)S(1)} %collective-permute-done.z_low.refs_0_, bf16[4,144,128]{2,1,0:T(8,128)(2,1)S(1)} %collective-permute-done.1.z_high.refs_1_, ...), custom_call_target="tpu_custom_call" | custom-call | flops 24999999488 | bytes 25000000 | tf_op jit(solution)/shard_map/near_middle/pallas_call | solution.py:492
  52.7 0.0 copy-start.7
  52.7 0.0 copy-start.9
  52.7 0.0 copy-start.10
  52.7 9.3 %widen.1.wide_hbm = bf16[7,2688,128]{2,1,0:T(8,128)(2,1)} custom-call(bf16[64,64,343]{2,1,0:T(8,128)(2,1)} %bitcast.48), custom_call_target="tpu_custom_call" | custom-call | flops 6000000000 | bytes 6000000 | tf_op jit(solution)/shard_map/widen/pallas_call | solution.py:557
  62.1 4.2 %collective-permute-done.5.refs_1_ = bf16[16,144,128]{2,1,0:T(8,128)(2,1)S(1)} collective-permute-done((bf16[16,144,128]{2,1,0:T(8,128)(2,1)S(1)}, bf16[16,144,128]{2,1,0:T(8,128)(2,1)S(1)}, u32[]{:S(2)}, u32[]{:S(2)}) %collective-permute-start.5) | collective-permute-done | bytes 589856 | tf_op jit(solution)/shard_map/ppermute | solution.py:54
  66.3 10.4 %near_last.1.near = f32[32,32,128]{2,1,0:T(8,128)S(1)} custom-call(s32[32,3]{1,0:T(8,128)S(1)} %copy-done.7, s32[8,9]{1,0:T(8,128)S(1)} %copy-done.9, s32[8,1]{1,0:T(8,128)S(1)} %copy-done.10, bf16[16,144,128]{2,1,0:T(8,128)(2,1)S(1)} %collective-permute-done.4.refs_0_, bf16[16,144,128]{2,1,0:T(8,128)(2,1)S(1)} %collective-permute-done.5.refs_1_, ...), custom_call_target="tpu_custom_call" | custom-call | flops 15000000512 | bytes 15000000 | tf_op jit(solution)/shard_map/near_last/pallas_call | solution.py:492
  76.7 0.8 copy-done.17
  77.4 21.4 %all-gather.3.cloned.1.call-done = bf16[4096,512]{1,0:T(8,128)(2,1)} async-done(((bf16[32,512]{1,0:T(8,128)(2,1)}), bf16[4096,512]{1,0:T(8,128)(2,1)}) %all-gather.3.cloned.1.call-update) | async-done | bytes 4194320 | tf_op jit(solution)/shard_map/all_gather | solution.py:530
  98.8 8.0 %far.1 = f32[8,32,512]{2,1,0:T(8,128)} custom-call(s32[8]{0:T(128)} %counts.3, bf16[64,2,32,512]{3,2,1,0:T(8,128)(2,1)} %bitcast.47, bf16[7,2688,128]{2,1,0:T(8,128)(2,1)} %widen.1.wide_hbm, bf16[8,64,64]{2,1,0:T(8,128)(2,1)} %up.1, bf16[8,64,64]{2,1,0:T(8,128)(2,1)} %down.1, bf16[8,64,512]{2,1,0:T(8,128)(2,1)} %get-tuple-element.49.shape, ...), custom_call_target="tpu_custom_call" | custom-call | flops 8000000000 | bytes 10000000 | tf_op jit(solution)/shard_map/far/pallas_call | solution.py:570
  (33 shorter events, 0.1 us)
Async XLA Ops:
  6.5 92.3 %all-gather.3.cloned.1.call-start = ((), (), s32[]{:S(2)}) async-start(), calls=%async_computation | async-start | bytes 4227072 | tf_op jit(solution)/shard_map/all_gather | solution.py:530
  6.5 10.2 %copy-start.6 = (s32[8]{0:T(128)S(1)}, s32[8]{0:T(128)}, u32[]{:S(2)}) copy-start(s32[8]{0:T(128)} %counts.3) | copy-start | bytes 100
  6.5 10.2 %copy-start.13 = (s32[8,3]{1,0:T(8,128)S(1)}, s32[8,3]{1,0:T(8,128)}, u32[]{:S(2)}) copy-start(s32[8,3]{1,0:T(8,128)} %constant.20.clone.leaves) | copy-start | bytes 292
  6.5 10.2 %copy-start.14 = (s32[1,8]{1,0:T(1,128)S(1)}, s32[1,8]{1,0:T(1,128)}, u32[]{:S(2)}) copy-start(s32[1,8]{1,0:T(1,128)} %constant.21.clone.sources) | copy-start | bytes 100
  6.5 10.2 %copy-start.16 = (s32[1,4]{1,0:T(1,128)S(1)}, s32[1,4]{1,0:T(1,128)}, u32[]{:S(2)}) copy-start(s32[1,4]{1,0:T(1,128)} %constant.22.clone.aims) | copy-start | bytes 52
  9.1 12.8 %collective-permute-start = (bf16[4,144,128]{2,1,0:T(8,128)(2,1)}, bf16[4,144,128]{2,1,0:T(8,128)(2,1)S(1)}, u32[]{:S(2)}, u32[]{:S(2)}) collective-permute-start(bf16[4,144,128]{2,1,0:T(8,128)(2,1)} %get-tuple-element.30.high.refs_1_), channel_id=1, source_target_pairs={{0,4},{1,5},{2,6},{3,7},{4,32},{5,33},{6,34},{7,35},{8,12},{9,13},... | collective-permute-start | bytes 442376 | tf_op jit(solution)/shard_map/ppermute | solution.py:54
  13.2 8.8 %collective-permute-start.1 = (bf16[4,144,128]{2,1,0:T(8,128)(2,1)}, bf16[4,144,128]{2,1,0:T(8,128)(2,1)S(1)}, u32[]{:S(2)}, u32[]{:S(2)}) collective-permute-start(bf16[4,144,128]{2,1,0:T(8,128)(2,1)} %get-tuple-element.31.low.refs_0_), channel_id=1, source_target_pairs={{4,0},{5,1},{6,2},{7,3},{12,8},{13,9},{14,10},{15,11},{20,16},{21,... | collective-permute-start | bytes 442376 | tf_op jit(solution)/shard_map/ppermute | solution.py:54
  14.5 0.9 copy-start
  15.4 0.9 copy-start.3
  16.7 0.9 copy-start.1
  17.6 0.9 copy-start.4
  18.6 8.2 %copy-start.15 = (s32[1,4]{1,0:T(1,128)S(1)}, s32[1,4]{1,0:T(1,128)}, u32[]{:S(2)}) copy-start(s32[1,4]{1,0:T(1,128)} %constant.23.clone.aims) | copy-start | bytes 52
  22.1 13.9 %copy-start.2 = (bf16[4,144,128]{2,1,0:T(8,128)(2,1)S(1)}, bf16[4,144,128]{2,1,0:T(8,128)(2,1)}, u32[]{:S(2)}) copy-start(bf16[4,144,128]{2,1,0:T(8,128)(2,1)} %get-tuple-element.31.low.refs_0_) | copy-start | bytes 442372
  22.1 13.9 %copy-start.5 = (bf16[4,144,128]{2,1,0:T(8,128)(2,1)S(1)}, bf16[4,144,128]{2,1,0:T(8,128)(2,1)}, u32[]{:S(2)}) copy-start(bf16[4,144,128]{2,1,0:T(8,128)(2,1)} %get-tuple-element.30.high.refs_1_) | copy-start | bytes 442372
  22.1 25.4 %copy-start.8 = (s32[24,3]{1,0:T(8,128)S(1)}, s32[24,3]{1,0:T(8,128)}, u32[]{:S(2)}) copy-start(s32[24,3]{1,0:T(8,128)} %constant.24.clone.leaves) | copy-start | bytes 868
  22.1 25.4 %copy-start.11 = (s32[6,6]{1,0:T(8,128)S(1)}, s32[6,6]{1,0:T(8,128)}, u32[]{:S(2)}) copy-start(s32[6,6]{1,0:T(8,128)} %constant.25.clone.sources) | copy-start | bytes 436
  22.1 25.4 %copy-start.12 = (s32[6,4]{1,0:T(8,128)S(1)}, s32[6,4]{1,0:T(8,128)}, u32[]{:S(2)}) copy-start(s32[6,4]{1,0:T(8,128)} %constant.26.clone.aims) | copy-start | bytes 292
  22.1 7.4 %collective-permute-start.2 = (bf16[8,144,128]{2,1,0:T(8,128)(2,1)S(1)}, bf16[8,144,128]{2,1,0:T(8,128)(2,1)S(1)}, u32[]{:S(2)}, u32[]{:S(2)}) collective-permute-start(bf16[8,144,128]{2,1,0:T(8,128)(2,1)S(1)} %bitcast.46), channel_id=1, source_target_pairs={{0,1},{1,8},{2,3},{3,10},{4,5},{5,12},{6,7},{7,14},{8,9},{9,64},{1... | collective-permute-start | bytes 884744 | tf_op jit(solution)/shard_map/ppermute | solution.py:54
  25.5 10.5 %collective-permute-start.3 = (bf16[8,144,128]{2,1,0:T(8,128)(2,1)S(1)}, bf16[8,144,128]{2,1,0:T(8,128)(2,1)S(1)}, u32[]{:S(2)}, u32[]{:S(2)}) collective-permute-start(bf16[8,144,128]{2,1,0:T(8,128)(2,1)S(1)} %bitcast.45), channel_id=1, source_target_pairs={{1,0},{3,2},{5,4},{7,6},{8,1},{9,8},{10,3},{11,10},{12,5},{13,12},... | collective-permute-start | bytes 884744 | tf_op jit(solution)/shard_map/ppermute | solution.py:54
  36.0 26.0 %collective-permute-start.4 = (bf16[16,144,128]{2,1,0:T(8,128)(2,1)S(1)}, bf16[16,144,128]{2,1,0:T(8,128)(2,1)S(1)}, u32[]{:S(2)}, u32[]{:S(2)}) collective-permute-start(bf16[16,144,128]{2,1,0:T(8,128)(2,1)S(1)} %get-tuple-element.46), channel_id=1, source_target_pairs={{0,2},{1,3},{2,16},{3,17},{4,6},{5,7},{6,20},{7,21},{8,10},{9,11},... | collective-permute-start | bytes 1769480 | tf_op jit(solution)/shard_map/ppermute | solution.py:54
  45.4 20.9 %collective-permute-start.5 = (bf16[16,144,128]{2,1,0:T(8,128)(2,1)S(1)}, bf16[16,144,128]{2,1,0:T(8,128)(2,1)S(1)}, u32[]{:S(2)}, u32[]{:S(2)}) collective-permute-start(bf16[16,144,128]{2,1,0:T(8,128)(2,1)S(1)} %get-tuple-element.47), channel_id=1, source_target_pairs={{2,0},{3,1},{6,4},{7,5},{10,8},{11,9},{14,12},{15,13},{16,2},{17,3... | collective-permute-start | bytes 1769480 | tf_op jit(solution)/shard_map/ppermute | solution.py:54
  52.7 13.6 %copy-start.7 = (s32[32,3]{1,0:T(8,128)S(1)}, s32[32,3]{1,0:T(8,128)}, u32[]{:S(2)}) copy-start(s32[32,3]{1,0:T(8,128)} %constant.27.clone.leaves) | copy-start | bytes 1156
  52.7 13.6 %copy-start.9 = (s32[8,9]{1,0:T(8,128)S(1)}, s32[8,9]{1,0:T(8,128)}, u32[]{:S(2)}) copy-start(s32[8,9]{1,0:T(8,128)} %constant.28.clone.sources) | copy-start | bytes 868
  52.7 13.6 %copy-start.10 = (s32[8,1]{1,0:T(8,128)S(1)}, s32[8,1]{1,0:T(8,128)}, u32[]{:S(2)}) copy-start(s32[8,1]{1,0:T(8,128)} %constant.29.clone.aims) | copy-start | bytes 100
  76.7 0.8 copy-start.17
Sparse Core Ops, SparseCore 0:
  10.5 88.2 all-gather.2
where the time goes:
time: 114 us
  Pallas kernels  42 us (37%)
  waiting for transfers between devices  32 us (28%)
  starting transfers between devices  21.4 us (19%)
  between operations  13.7 us (12%)
  local copies, waits for them, and re-layouts  4.52 us (4%)
    pallas_call x4, Pallas kernels, near_call(): call(functools.partial(near_kernel, sides, before is not None), [SMEM] *...  21.6 us
    ppermute x6, starting transfers between devices, shifted(): return lax.ppermute(value, AXES, pairs)  21.4 us
    all_gather x1, waiting for transfers between devices, per_device(): gathered = lax.all_gather(equiv, AXES, axis=0)  21.4 us
    ppermute x6, waiting for transfers between devices, shifted(): return lax.ppermute(value, AXES, pairs)  10.6 us
    pallas_call x1, Pallas kernels, per_device(): call(widen_kernel, [VMEM], shape_of((7, 7 * 6 * 64, 128), BF16), [pltpu.V...  9.34 us
    pallas_call x1, Pallas kernels, per_device(): call(functools.partial(far_kernel, total_bits), [SMEM, anywhere, anywhere...  8.05 us
    unnamed x36, local copies, waits for them, and re-layouts  4.47 us
    pallas_call x1, Pallas kernels, per_device(): call(upward_kernel, [SMEM, VMEM, VMEM, VMEM], (half, half, shape_of((8, 6...  2.53 us
  transfers between devices with their start and end apart: 7, of which 3 were waited for; matrix products, arithmetic and copies ran while one was open for 0% of the time, Pallas kernels for 28%

commit v1 on v0

--- a/solution.py
+++ b/solution.py
@@ -2,7 +2,6 @@
 
 import jax
 import jax.numpy as jnp
-import numpy as np
 from jax import lax
 from jax.experimental import pallas as pl
 from jax.experimental.pallas import tpu as pltpu
@@ -139,22 +138,17 @@
     equiv_out[...] = jnp.concatenate([equiv[32 * l : 32 * l + 32] for l in range(8)], 1)
 
 
-def targets_kernel(low, high, targets):
-    for leaf in range(8):
-        src, at = (low, leaf) if leaf < 4 else (high, leaf - 4)
-        offsets = (leaf % 2 - 1.0, leaf // 2 % 2 - 1.0, leaf // 4 - 1.0)
-        block = src[at, 128:144, :].astype(F32)
-        for j in range(4):
-            features = target_features(block[4 * j : 4 * j + 4], offsets)
-            targets[4 * leaf + j] = features.T.astype(BF16)
-
-
-def near_kernel(sides, with_before, leaves, sources, aims, *refs):
+def near_kernel(sides, opens, tables, *refs):
     payloads, refs = refs[: len(sides)], refs[len(sides) :]
-    targets, refs = refs[0], refs[1:]
-    if with_before:
-        before, refs = refs[0], refs[1:]
-    counts, out, features, values, live_v, live_s, queue, aim_queue, sem = refs
+    if opens:
+        counts, out, targets, low, high, *refs = refs
+    else:
+        targets, before, counts, out, *refs = refs
+    features, values, live_v, live_s, queue, aim_queue, leaves, sources, aims = refs
+    for table, ref in zip(tables, (leaves, sources, aims)):
+        for i, row in enumerate(table):
+            for k, entry in enumerate(row):
+                ref[i, k] = jnp.int32(entry)
     n_leaves = sum(sides)
     n_tasks, n_sources = sources.shape
     n_aims = aims.shape[1]
@@ -177,10 +171,20 @@
         first += size
     features[4 * n_leaves] = features[0]
     values[4 * n_leaves] = jnp.zeros((32, CHUNK), BF16)
-    copy = pltpu.make_async_copy(live_v, live_s, sem)
-    copy.start()
-    copy.wait()
-    out[...] = before[...] if with_before else jnp.zeros_like(out)
+    for at in range(n_leaves):
+        live_s[at] = live_v[at : at + 1, :][0, 0]
+    if opens:
+        out[...] = jnp.zeros_like(out)
+        low[...] = payloads[0][...]
+        high[...] = payloads[1][...]
+        for leaf in range(8):
+            block = payloads[leaf // 4][leaf % 4, 128:144, :].astype(F32)
+            offsets = (leaf % 2 - 1.0, leaf // 2 % 2 - 1.0, leaf // 4 - 1.0)
+            for j in range(4):
+                rows = target_features(block[4 * j : 4 * j + 4], offsets)
+                targets[4 * leaf + j] = rows.T.astype(BF16)
+    else:
+        out[...] = before[...]
 
     def compute(start, n_rows, n_items):
         places = [aim_queue[start + i] for i in range(n_rows)]
@@ -216,7 +220,7 @@
         n_items = jnp.int32(0)
         for k in range(n_sources):
             leaf = sources[i, k]
-            n_live = jnp.where(leaf >= 0, live_s[jnp.maximum(leaf, 0), 0], 0)
+            n_live = jnp.where(leaf >= 0, live_s[jnp.maximum(leaf, 0)], 0)
             for j in range(4):
                 queue[n_items] = 4 * leaf + j
                 n_items = n_items + (j < n_live).astype(jnp.int32)
@@ -265,7 +269,7 @@
     n_offsets = table.shape[2]
     n_lanes = 3 * CHUNK
     stride = n_equiv + 1
-    together = 8
+    together = 16
     unit = row_index((CHUNK, CHUNK)) == lax.broadcasted_iota(jnp.int32, (CHUNK, CHUNK), 1)
     unit = jnp.where(unit, 1.0, 0.0).astype(BF16)
 
@@ -480,27 +484,32 @@
     n_aims = max(len(task[1]) for task in tasks)
     pad = lambda row, size: row + [-1] * (size - len(row))
     tables = [
-        np.array(places, np.int32) - 2,
-        np.array([pad(task[0], n_sources) for task in tasks], np.int32),
-        np.array([pad(task[1], n_aims) for task in tasks], np.int32),
+        [[c - 2 for c in place] for place in places],
+        [pad(task[0], n_sources) for task in tasks],
+        [pad(task[1], n_aims) for task in tasks],
     ]
-    args = [jnp.asarray(table) for table in tables] + list(payloads) + [targets]
-    if before is not None:
-        args.append(before)
+    opens = before is None
+    args = list(payloads)
+    outs = jax.ShapeDtypeStruct((32, 32, CHUNK), F32)
+    if opens:
+        half = jax.ShapeDtypeStruct(payloads[0].shape, BF16)
+        outs = (outs, jax.ShapeDtypeStruct((32, CHUNK, FEATURES), BF16), half, half)
+    else:
+        args += [targets, before]
     args.append(counts)
     us = {"first": 12, "second": 12, "middle": 25, "last": 15}[phase]
     return call(
-        functools.partial(near_kernel, sides, before is not None),
-        [SMEM] * 3 + [VMEM] * (len(args) - 4) + [SMEM],
-        jax.ShapeDtypeStruct((32, 32, CHUNK), F32),
+        functools.partial(near_kernel, sides, opens, tables),
+        [VMEM] * (len(args) - 1) + [SMEM],
+        outs,
         [
             pltpu.VMEM((4 * n_leaves + 1, FEATURES, CHUNK), BF16),
             pltpu.VMEM((4 * n_leaves + 1, 32, CHUNK), BF16),
             pltpu.VMEM((n_leaves, CHUNK), jnp.int32),
-            pltpu.SMEM((n_leaves, CHUNK), jnp.int32),
+            pltpu.SMEM((n_leaves,), jnp.int32),
             pltpu.SMEM((64,), jnp.int32),
             pltpu.SMEM((40,), jnp.int32),
-            pltpu.SemaphoreType.DMA,
+            *[pltpu.SMEM((len(table), len(table[0])), jnp.int32) for table in tables],
         ],
         flops=us * 10**9,
         seen=us * 10**6,
@@ -528,15 +537,7 @@
     z_low = move(high, 2, 1)
     z_high = move(low, 2, -1)
     gathered = lax.all_gather(equiv, AXES, axis=0)
-    targets = call(
-        targets_kernel,
-        [VMEM] * 2,
-        shape_of((32, CHUNK, FEATURES), BF16),
-        seen=10**6,
-        flops=10**9,
-        name="targets",
-    )(low, high)
-    near = near_call("first", (low, high), targets, counts, None)
+    near, targets, low, high = near_call("first", (low, high), None, counts, None)
     z_low, z_high, near = lax.optimization_barrier((z_low, z_high, near))
     planes = [a.reshape(2, 2, ROWS, CHUNK) for a in (z_low, low, high, z_high)]
     faces = [jnp.stack([a[:, x] for a in planes]).reshape(8, ROWS, CHUNK) for x in range(2)]

time: 114 us -> 111 us (0.974); the launches traced: 114 us -> 112 us
  Pallas kernels: 42 us -> 48.1 us
  waiting for transfers between devices: 32 us -> 27.1 us
  local copies, waits for them, and re-layouts: 4.52 us -> 2.68 us
    ppermute x6, waiting for transfers between devices: 10.6 us -> 3.21 us  [shifted(): return lax.ppermute(value, AXES, pairs)]
    pallas_call x5 -> x4, Pallas kernels: 22 us -> 29 us  [near_call(): call(functools.partial(near_kernel, sides, opens, tables), [VMEM] * (len(...]
    all_gather x1, waiting for transfers between devices: 21.4 us -> 23.9 us  [per_device(): gathered = lax.all_gather(equiv, AXES, axis=0)]
    unnamed x36 -> x8, local copies, waits for them, and re-layouts: 4.47 us -> 2.63 us
  transfers between devices with their start and end apart: 7 -> 7, of which waited for: 3 -> 2; matrix products, arithmetic and copies ran while one was open for 0% -> 0% of each run, Pallas kernels for 28% -> 34%
where the time goes in v1:
time: 111 us; the launch traced here: 112 us
  Pallas kernels  48.1 us (43%)
  waiting for transfers between devices  27.1 us (24%)
  starting transfers between devices  20.4 us (18%)
  between operations  13.6 us (12%)
  local copies, waits for them, and re-layouts  2.68 us (2%)
    pallas_call x4, Pallas kernels, near_call(): call(functools.partial(near_kernel, sides, opens, tables), [VMEM] * (len(...  29 us
    all_gather x1, waiting for transfers between devices, per_device(): gathered = lax.all_gather(equiv, AXES, axis=0)  23.9 us
    ppermute x6, starting transfers between devices, shifted(): return lax.ppermute(value, AXES, pairs)  20.4 us
    pallas_call x1, Pallas kernels, per_device(): call(widen_kernel, [VMEM], shape_of((7, 7 * 6 * 64, 128), BF16), [pltpu.V...  8.45 us
    pallas_call x1, Pallas kernels, per_device(): call(functools.partial(far_kernel, total_bits), [SMEM, anywhere, anywhere...  8.05 us
    ppermute x6, waiting for transfers between devices, shifted(): return lax.ppermute(value, AXES, pairs)  3.21 us
    unnamed x8, local copies, waits for them, and re-layouts  2.63 us
    pallas_call x1, Pallas kernels, per_device(): call(upward_kernel, [SMEM, VMEM, VMEM, VMEM], (half, half, shape_of((8, 6...  2.5 us
  transfers between devices with their start and end apart: 7, of which 2 were waited for; matrix products, arithmetic and copies ran while one was open for 0% of the time, Pallas kernels for 34%

profile of v1, /device:TPU:1, one launch (start us, length us, event | category | flops | bytes accessed | tf_op | source)
XLA Modules:
  0.0 111.9 jit_solution(3657760907309279892)
XLA Ops:
  6.5 0.0 all-gather.3.cloned.1.call-start
  6.5 0.0 copy-start.2
  6.5 2.5 %upward.1 = (bf16[4,144,128]{2,1,0:T(8,128)(2,1)}, bf16[4,144,128]{2,1,0:T(8,128)(2,1)}, bf16[8,64,512]{2,1,0:T(8,128)(2,1)}, bf16[32,512]{1,0:T(8,128)(2,1)}) custom-call(s32[8]{0:T(128)} %counts.3, bf16[3,8,512]{2,1,0:T(8,128)(2,1)} %bitcast.49, bf16[8,32,512]{2,1,0:T(8,128)(2,1)} %charges.1, bf16[64,64]{1,0:T(8,128)(2,1)} %to_equiv.1), custom_call_target="tpu_custom_call" | custom-call | flops 3000000000 | bytes 3000000 | tf_op jit(solution)/shard_map/upward/pallas_call | solution.py:527
  9.0 0.0 all-gather.3.cloned.1.call-update
  9.1 4.0 %collective-permute-start = (bf16[4,144,128]{2,1,0:T(8,128)(2,1)}, bf16[4,144,128]{2,1,0:T(8,128)(2,1)S(1)}, u32[]{:S(2)}, u32[]{:S(2)}) collective-permute-start(bf16[4,144,128]{2,1,0:T(8,128)(2,1)} %get-tuple-element.34.refs_1_), channel_id=1, source_target_pairs={{0,4},{1,5},{2,6},{3,7},{4,32},{5,33},{6,34},{7,35},{8,12},{9,13},... | collective-permute-start | bytes 442376 | tf_op jit(solution)/shard_map/ppermute | solution.py:53
  13.1 1.3 %collective-permute-start.1 = (bf16[4,144,128]{2,1,0:T(8,128)(2,1)}, bf16[4,144,128]{2,1,0:T(8,128)(2,1)S(1)}, u32[]{:S(2)}, u32[]{:S(2)}) collective-permute-start(bf16[4,144,128]{2,1,0:T(8,128)(2,1)} %get-tuple-element.35.refs_0_), channel_id=1, source_target_pairs={{4,0},{5,1},{6,2},{7,3},{12,8},{13,9},{14,10},{15,11},{20,16},{21,... | collective-permute-start | bytes 442376 | tf_op jit(solution)/shard_map/ppermute | solution.py:53
  14.4 0.0 copy-done.2
  14.4 0.0 copy-start
  14.4 0.9 copy-done
  15.3 0.0 copy-start.1
  15.3 0.9 copy-done.1
  16.2 4.5 %near_first.1 = (f32[32,32,128]{2,1,0:T(8,128)S(1)}, bf16[32,128,48]{2,1,0:T(8,128)(2,1)S(1)}, bf16[4,144,128]{2,1,0:T(8,128)(2,1)S(1)}, bf16[4,144,128]{2,1,0:T(8,128)(2,1)S(1)}) custom-call(bf16[4,144,128]{2,1,0:T(8,128)(2,1)S(1)} %copy-done, bf16[4,144,128]{2,1,0:T(8,128)(2,1)S(1)} %copy-done.1, s32[8]{0:T(128)S(1)} %copy-done.2), custom_call_target="tpu_custom_call" | custom-call | flops 12000000000 | bytes 12000000 | tf_op jit(solution)/shard_map/near_first/pallas_call | solution.py:501
  20.8 0.0 collective-permute-done.z_low.refs_0_
  20.8 0.0 collective-permute-done.1.z_high.refs_1_
  20.9 0.1 pad_maximum_fusion
  20.9 4.1 %collective-permute-start.2 = (bf16[8,144,128]{2,1,0:T(8,128)(2,1)S(1)}, bf16[8,144,128]{2,1,0:T(8,128)(2,1)S(1)}, u32[]{:S(2)}, u32[]{:S(2)}) collective-permute-start(bf16[8,144,128]{2,1,0:T(8,128)(2,1)S(1)} %bitcast.46), channel_id=1, source_target_pairs={{0,1},{1,8},{2,3},{3,10},{4,5},{5,12},{6,7},{7,14},{8,9},{9,64},{1... | collective-permute-start | bytes 884744 | tf_op jit(solution)/shard_map/ppermute | solution.py:53
  25.1 1.3 %collective-permute-start.3 = (bf16[8,144,128]{2,1,0:T(8,128)(2,1)S(1)}, bf16[8,144,128]{2,1,0:T(8,128)(2,1)S(1)}, u32[]{:S(2)}, u32[]{:S(2)}) collective-permute-start(bf16[8,144,128]{2,1,0:T(8,128)(2,1)S(1)} %bitcast.45), channel_id=1, source_target_pairs={{1,0},{3,2},{5,4},{7,6},{8,1},{9,8},{10,3},{11,10},{12,5},{13,12},... | collective-permute-start | bytes 884744 | tf_op jit(solution)/shard_map/ppermute | solution.py:53
  26.4 5.6 %near_second.1.refs_5_ = f32[32,32,128]{2,1,0:T(8,128)S(1)} custom-call(bf16[4,144,128]{2,1,0:T(8,128)(2,1)S(1)} %get-tuple-element.39.refs_0_.low, bf16[4,144,128]{2,1,0:T(8,128)(2,1)S(1)} %get-tuple-element.40.refs_1_.high, bf16[32,128,48]{2,1,0:T(8,128)(2,1)S(1)} %get-tuple-element.44.refs_2_.refs_4_, f32[32,32,128]{2,1,0:T(8,128)S(1)} %get-tuple-element.45.refs_3_, ...), custom_call_target="tpu_custom_call" | custom-call | flops 12000000000 | bytes 12000000 | tf_op jit(solution)/shard_map/near_second/pallas_call | solution.py:501
  32.0 0.0 collective-permute-done.2.x_low.refs_2_
  32.0 3.2 %collective-permute-done.3.x_high.refs_3_ = bf16[8,144,128]{2,1,0:T(8,128)(2,1)S(1)} collective-permute-done((bf16[8,144,128]{2,1,0:T(8,128)(2,1)S(1)}, bf16[8,144,128]{2,1,0:T(8,128)(2,1)S(1)}, u32[]{:S(2)}, u32[]{:S(2)}) %collective-permute-start.3) | collective-permute-done | bytes 294944 | tf_op jit(solution)/shard_map/ppermute | solution.py:53
  35.2 0.1 faces.1
  35.2 5.5 %collective-permute-start.4 = (bf16[16,144,128]{2,1,0:T(8,128)(2,1)S(1)}, bf16[16,144,128]{2,1,0:T(8,128)(2,1)S(1)}, u32[]{:S(2)}, u32[]{:S(2)}) collective-permute-start(bf16[16,144,128]{2,1,0:T(8,128)(2,1)S(1)} %get-tuple-element.54), channel_id=1, source_target_pairs={{0,2},{1,3},{2,16},{3,17},{4,6},{5,7},{6,20},{7,21},{8,10},{9,11},... | collective-permute-start | bytes 1769480 | tf_op jit(solution)/shard_map/ppermute | solution.py:53
  40.8 4.1 %collective-permute-start.5 = (bf16[16,144,128]{2,1,0:T(8,128)(2,1)S(1)}, bf16[16,144,128]{2,1,0:T(8,128)(2,1)S(1)}, u32[]{:S(2)}, u32[]{:S(2)}) collective-permute-start(bf16[16,144,128]{2,1,0:T(8,128)(2,1)S(1)} %get-tuple-element.55), channel_id=1, source_target_pairs={{2,0},{3,1},{6,4},{7,5},{10,8},{11,9},{14,12},{15,13},{16,2},{17,3... | collective-permute-start | bytes 1769480 | tf_op jit(solution)/shard_map/ppermute | solution.py:53
  44.9 8.3 %near_middle.1.refs_3_ = f32[32,32,128]{2,1,0:T(8,128)S(1)} custom-call(bf16[4,144,128]{2,1,0:T(8,128)(2,1)S(1)} %collective-permute-done.z_low.refs_0_, bf16[4,144,128]{2,1,0:T(8,128)(2,1)S(1)} %collective-permute-done.1.z_high.refs_1_, bf16[8,144,128]{2,1,0:T(8,128)(2,1)S(1)} %collective-permute-done.2.x_low.refs_2_, ...), custom_call_target="tpu_custom_call" | custom-call | flops 24999999488 | bytes 25000000 | tf_op jit(solution)/shard_map/near_middle/pallas_call | solution.py:501
  53.1 8.5 %widen.1.wide_hbm = bf16[7,2688,128]{2,1,0:T(8,128)(2,1)} custom-call(bf16[64,64,343]{2,1,0:T(8,128)(2,1)} %bitcast.48), custom_call_target="tpu_custom_call" | custom-call | flops 6000000000 | bytes 6000000 | tf_op jit(solution)/shard_map/widen/pallas_call | solution.py:558
  61.6 0.0 collective-permute-done.4.refs_0_
  61.6 0.0 collective-permute-done.5.refs_1_
  61.6 10.7 %near_last.1.near = f32[32,32,128]{2,1,0:T(8,128)S(1)} custom-call(bf16[16,144,128]{2,1,0:T(8,128)(2,1)S(1)} %collective-permute-done.4.refs_0_, bf16[16,144,128]{2,1,0:T(8,128)(2,1)S(1)} %collective-permute-done.5.refs_1_, bf16[32,128,48]{2,1,0:T(8,128)(2,1)S(1)} %get-tuple-element.44.refs_2_.refs_4_, f32[32,32,128]{2,1,0:T(8,128)S(1)} %near_middle.1.refs_3_, ...), custom_call_target="tpu_custom_call" | custom-call | flops 15000000512 | bytes 15000000 | tf_op jit(solution)/shard_map/near_last/pallas_call | solution.py:501
  72.3 0.0 copy-start.3
  72.3 0.8 copy-done.3
  73.1 23.9 %all-gather.3.cloned.1.call-done = bf16[4096,512]{1,0:T(8,128)(2,1)} async-done(((bf16[32,512]{1,0:T(8,128)(2,1)}), bf16[4096,512]{1,0:T(8,128)(2,1)}) %all-gather.3.cloned.1.call-update) | async-done | bytes 4194320 | tf_op jit(solution)/shard_map/all_gather | solution.py:539
  97.0 8.0 %far.1 = f32[8,32,512]{2,1,0:T(8,128)} custom-call(s32[8]{0:T(128)} %counts.3, bf16[64,2,32,512]{3,2,1,0:T(8,128)(2,1)} %bitcast.47, bf16[7,2688,128]{2,1,0:T(8,128)(2,1)} %widen.1.wide_hbm, bf16[8,64,64]{2,1,0:T(8,128)(2,1)} %up.1, bf16[8,64,64]{2,1,0:T(8,128)(2,1)} %down.1, bf16[8,64,512]{2,1,0:T(8,128)(2,1)} %get-tuple-element.57.shape, ...), custom_call_target="tpu_custom_call" | custom-call | flops 8000000000 | bytes 10000000 | tf_op jit(solution)/shard_map/far/pallas_call | solution.py:571
  (4 shorter events, 0.0 us)
Async XLA Ops:
  6.5 90.5 %all-gather.3.cloned.1.call-start = ((), (), s32[]{:S(2)}) async-start(), calls=%async_computation | async-start | bytes 4227072 | tf_op jit(solution)/shard_map/all_gather | solution.py:539
  6.5 7.9 %copy-start.2 = (s32[8]{0:T(128)S(1)}, s32[8]{0:T(128)}, u32[]{:S(2)}) copy-start(s32[8]{0:T(128)} %counts.3) | copy-start | bytes 100
  9.1 11.7 %collective-permute-start = (bf16[4,144,128]{2,1,0:T(8,128)(2,1)}, bf16[4,144,128]{2,1,0:T(8,128)(2,1)S(1)}, u32[]{:S(2)}, u32[]{:S(2)}) collective-permute-start(bf16[4,144,128]{2,1,0:T(8,128)(2,1)} %get-tuple-element.34.refs_1_), channel_id=1, source_target_pairs={{0,4},{1,5},{2,6},{3,7},{4,32},{5,33},{6,34},{7,35},{8,12},{9,13},... | collective-permute-start | bytes 442376 | tf_op jit(solution)/shard_map/ppermute | solution.py:53
  13.1 7.7 %collective-permute-start.1 = (bf16[4,144,128]{2,1,0:T(8,128)(2,1)}, bf16[4,144,128]{2,1,0:T(8,128)(2,1)S(1)}, u32[]{:S(2)}, u32[]{:S(2)}) collective-permute-start(bf16[4,144,128]{2,1,0:T(8,128)(2,1)} %get-tuple-element.35.refs_0_), channel_id=1, source_target_pairs={{4,0},{5,1},{6,2},{7,3},{12,8},{13,9},{14,10},{15,11},{20,16},{21,... | collective-permute-start | bytes 442376 | tf_op jit(solution)/shard_map/ppermute | solution.py:53
  14.4 0.9 copy-start
  15.3 0.9 copy-start.1
  20.9 11.0 %collective-permute-start.2 = (bf16[8,144,128]{2,1,0:T(8,128)(2,1)S(1)}, bf16[8,144,128]{2,1,0:T(8,128)(2,1)S(1)}, u32[]{:S(2)}, u32[]{:S(2)}) collective-permute-start(bf16[8,144,128]{2,1,0:T(8,128)(2,1)S(1)} %bitcast.46), channel_id=1, source_target_pairs={{0,1},{1,8},{2,3},{3,10},{4,5},{5,12},{6,7},{7,14},{8,9},{9,64},{1... | collective-permute-start | bytes 884744 | tf_op jit(solution)/shard_map/ppermute | solution.py:53
  25.1 10.1 %collective-permute-start.3 = (bf16[8,144,128]{2,1,0:T(8,128)(2,1)S(1)}, bf16[8,144,128]{2,1,0:T(8,128)(2,1)S(1)}, u32[]{:S(2)}, u32[]{:S(2)}) collective-permute-start(bf16[8,144,128]{2,1,0:T(8,128)(2,1)S(1)} %bitcast.45), channel_id=1, source_target_pairs={{1,0},{3,2},{5,4},{7,6},{8,1},{9,8},{10,3},{11,10},{12,5},{13,12},... | collective-permute-start | bytes 884744 | tf_op jit(solution)/shard_map/ppermute | solution.py:53
  35.2 26.3 %collective-permute-start.4 = (bf16[16,144,128]{2,1,0:T(8,128)(2,1)S(1)}, bf16[16,144,128]{2,1,0:T(8,128)(2,1)S(1)}, u32[]{:S(2)}, u32[]{:S(2)}) collective-permute-start(bf16[16,144,128]{2,1,0:T(8,128)(2,1)S(1)} %get-tuple-element.54), channel_id=1, source_target_pairs={{0,2},{1,3},{2,16},{3,17},{4,6},{5,7},{6,20},{7,21},{8,10},{9,11},... | collective-permute-start | bytes 1769480 | tf_op jit(solution)/shard_map/ppermute | solution.py:53
  40.8 20.9 %collective-permute-start.5 = (bf16[16,144,128]{2,1,0:T(8,128)(2,1)S(1)}, bf16[16,144,128]{2,1,0:T(8,128)(2,1)S(1)}, u32[]{:S(2)}, u32[]{:S(2)}) collective-permute-start(bf16[16,144,128]{2,1,0:T(8,128)(2,1)S(1)} %get-tuple-element.55), channel_id=1, source_target_pairs={{2,0},{3,1},{6,4},{7,5},{10,8},{11,9},{14,12},{15,13},{16,2},{17,3... | collective-permute-start | bytes 1769480 | tf_op jit(solution)/shard_map/ppermute | solution.py:53
  72.3 0.8 copy-start.3
Sparse Core Ops, SparseCore 0:
  10.5 86.4 all-gather.2

commit v2 on v1

--- a/solution.py
+++ b/solution.py
@@ -559,7 +559,7 @@
         widen_kernel,
         [VMEM],
         shape_of((7, 7 * 6 * 64, 128), BF16),
-        [pltpu.VMEM((3 * CHUNK * 65, 128), F32)],
+        [pltpu.VMEM((3 * CHUNK * 65 + CHUNK, 128), F32)],
         limit=56,
         seen=6 * 10**6,
         flops=6 * 10**9,

time: 111 us -> 112 us (level); the launches traced: 112 us -> 111 us
  waiting for transfers between devices: 27.1 us -> 33.5 us
  Pallas kernels: 48.1 us -> 42.6 us
  starting transfers between devices: 20.4 us -> 18.1 us
    ppermute x6, waiting for transfers between devices: 3.21 us -> 8.96 us  [shifted(): return lax.ppermute(value, AXES, pairs)]
    pallas_call x4, Pallas kernels: 29 us -> 23.5 us  [near_call(): call(functools.partial(near_kernel, sides, opens, tables), [VMEM] * (len(...]
    ppermute x6, starting transfers between devices: 20.4 us -> 18.1 us  [shifted(): return lax.ppermute(value, AXES, pairs)]
  transfers between devices with their start and end apart: 7 -> 7, of which waited for: 2 -> 2; matrix products, arithmetic and copies ran while one was open for 0% -> 0% of each run, Pallas kernels for 34% -> 29%
where the time goes in v2:
time: 112 us; the launch traced here: 111 us
  Pallas kernels  42.6 us (38%)
  waiting for transfers between devices  33.5 us (30%)
  starting transfers between devices  18.1 us (16%)
  between operations  13.6 us (12%)
  local copies, waits for them, and re-layouts  2.66 us (2%)
    all_gather x1, waiting for transfers between devices, per_device(): gathered = lax.all_gather(equiv, AXES, axis=0)  24.5 us
    pallas_call x4, Pallas kernels, near_call(): call(functools.partial(near_kernel, sides, opens, tables), [VMEM] * (len(...  23.5 us
    ppermute x6, starting transfers between devices, shifted(): return lax.ppermute(value, AXES, pairs)  18.1 us
    ppermute x6, waiting for transfers between devices, shifted(): return lax.ppermute(value, AXES, pairs)  8.96 us
    pallas_call x1, Pallas kernels, per_device(): call(widen_kernel, [VMEM], shape_of((7, 7 * 6 * 64, 128), BF16), [pltpu.V...  8.47 us
    pallas_call x1, Pallas kernels, per_device(): call(functools.partial(far_kernel, total_bits), [SMEM, anywhere, anywhere...  8.04 us
    unnamed x8, local copies, waits for them, and re-layouts  2.61 us
    pallas_call x1, Pallas kernels, per_device(): call(upward_kernel, [SMEM, VMEM, VMEM, VMEM], (half, half, shape_of((8, 6...  2.5 us
  transfers between devices with their start and end apart: 7, of which 2 were waited for; matrix products, arithmetic and copies ran while one was open for 0% of the time, Pallas kernels for 29%

profile of v2, /device:TPU:1, one launch (start us, length us, event | category | flops | bytes accessed | tf_op | source)
XLA Modules:
  0.0 110.5 jit_solution(2854452916276513733)
XLA Ops:
  6.5 0.0 all-gather.3.cloned.1.call-start
  6.5 0.0 copy-start.2
  6.5 2.5 %upward.1 = (bf16[4,144,128]{2,1,0:T(8,128)(2,1)}, bf16[4,144,128]{2,1,0:T(8,128)(2,1)}, bf16[8,64,512]{2,1,0:T(8,128)(2,1)}, bf16[32,512]{1,0:T(8,128)(2,1)}) custom-call(s32[8]{0:T(128)} %counts.3, bf16[3,8,512]{2,1,0:T(8,128)(2,1)} %bitcast.49, bf16[8,32,512]{2,1,0:T(8,128)(2,1)} %charges.1, bf16[64,64]{1,0:T(8,128)(2,1)} %to_equiv.1), custom_call_target="tpu_custom_call" | custom-call | flops 3000000000 | bytes 3000000 | tf_op jit(solution)/shard_map/upward/pallas_call | solution.py:527
  9.0 0.0 all-gather.3.cloned.1.call-update
  9.1 4.0 %collective-permute-start = (bf16[4,144,128]{2,1,0:T(8,128)(2,1)}, bf16[4,144,128]{2,1,0:T(8,128)(2,1)S(1)}, u32[]{:S(2)}, u32[]{:S(2)}) collective-permute-start(bf16[4,144,128]{2,1,0:T(8,128)(2,1)} %get-tuple-element.34.refs_1_), channel_id=1, source_target_pairs={{0,4},{1,5},{2,6},{3,7},{4,32},{5,33},{6,34},{7,35},{8,12},{9,13},... | collective-permute-start | bytes 442376 | tf_op jit(solution)/shard_map/ppermute | solution.py:53
  13.1 1.3 %collective-permute-start.1 = (bf16[4,144,128]{2,1,0:T(8,128)(2,1)}, bf16[4,144,128]{2,1,0:T(8,128)(2,1)S(1)}, u32[]{:S(2)}, u32[]{:S(2)}) collective-permute-start(bf16[4,144,128]{2,1,0:T(8,128)(2,1)} %get-tuple-element.35.refs_0_), channel_id=1, source_target_pairs={{4,0},{5,1},{6,2},{7,3},{12,8},{13,9},{14,10},{15,11},{20,16},{21,... | collective-permute-start | bytes 442376 | tf_op jit(solution)/shard_map/ppermute | solution.py:53
  14.4 0.0 copy-done.2
  14.4 0.0 copy-start
  14.4 0.9 copy-done
  15.3 0.0 copy-start.1
  15.3 0.9 copy-done.1
  16.2 3.8 %near_first.1 = (f32[32,32,128]{2,1,0:T(8,128)S(1)}, bf16[32,128,48]{2,1,0:T(8,128)(2,1)S(1)}, bf16[4,144,128]{2,1,0:T(8,128)(2,1)S(1)}, bf16[4,144,128]{2,1,0:T(8,128)(2,1)S(1)}) custom-call(bf16[4,144,128]{2,1,0:T(8,128)(2,1)S(1)} %copy-done, bf16[4,144,128]{2,1,0:T(8,128)(2,1)S(1)} %copy-done.1, s32[8]{0:T(128)S(1)} %copy-done.2), custom_call_target="tpu_custom_call" | custom-call | flops 12000000000 | bytes 12000000 | tf_op jit(solution)/shard_map/near_first/pallas_call | solution.py:501
  20.1 0.0 collective-permute-done.z_low.refs_0_
  20.2 0.0 collective-permute-done.1.z_high.refs_1_
  20.2 0.1 pad_maximum_fusion
  20.3 3.1 %collective-permute-start.2 = (bf16[8,144,128]{2,1,0:T(8,128)(2,1)S(1)}, bf16[8,144,128]{2,1,0:T(8,128)(2,1)S(1)}, u32[]{:S(2)}, u32[]{:S(2)}) collective-permute-start(bf16[8,144,128]{2,1,0:T(8,128)(2,1)S(1)} %bitcast.46), channel_id=1, source_target_pairs={{0,1},{1,8},{2,3},{3,10},{4,5},{5,12},{6,7},{7,14},{8,9},{9,64},{1... | collective-permute-start | bytes 884744 | tf_op jit(solution)/shard_map/ppermute | solution.py:53
  23.4 1.3 %collective-permute-start.3 = (bf16[8,144,128]{2,1,0:T(8,128)(2,1)S(1)}, bf16[8,144,128]{2,1,0:T(8,128)(2,1)S(1)}, u32[]{:S(2)}, u32[]{:S(2)}) collective-permute-start(bf16[8,144,128]{2,1,0:T(8,128)(2,1)S(1)} %bitcast.45), channel_id=1, source_target_pairs={{1,0},{3,2},{5,4},{7,6},{8,1},{9,8},{10,3},{11,10},{12,5},{13,12},... | collective-permute-start | bytes 884744 | tf_op jit(solution)/shard_map/ppermute | solution.py:53
  24.7 4.0 %near_second.1.refs_5_ = f32[32,32,128]{2,1,0:T(8,128)S(1)} custom-call(bf16[4,144,128]{2,1,0:T(8,128)(2,1)S(1)} %get-tuple-element.39.refs_0_.low, bf16[4,144,128]{2,1,0:T(8,128)(2,1)S(1)} %get-tuple-element.40.refs_1_.high, bf16[32,128,48]{2,1,0:T(8,128)(2,1)S(1)} %get-tuple-element.44.refs_2_.refs_4_, f32[32,32,128]{2,1,0:T(8,128)S(1)} %get-tuple-element.45.refs_3_, ...), custom_call_target="tpu_custom_call" | custom-call | flops 12000000000 | bytes 12000000 | tf_op jit(solution)/shard_map/near_second/pallas_call | solution.py:501
  28.6 0.0 collective-permute-done.2.x_low.refs_2_
  28.7 8.9 %collective-permute-done.3.x_high.refs_3_ = bf16[8,144,128]{2,1,0:T(8,128)(2,1)S(1)} collective-permute-done((bf16[8,144,128]{2,1,0:T(8,128)(2,1)S(1)}, bf16[8,144,128]{2,1,0:T(8,128)(2,1)S(1)}, u32[]{:S(2)}, u32[]{:S(2)}) %collective-permute-start.3) | collective-permute-done | bytes 294944 | tf_op jit(solution)/shard_map/ppermute | solution.py:53
  37.6 0.1 faces.1
  37.7 2.6 %collective-permute-start.4 = (bf16[16,144,128]{2,1,0:T(8,128)(2,1)S(1)}, bf16[16,144,128]{2,1,0:T(8,128)(2,1)S(1)}, u32[]{:S(2)}, u32[]{:S(2)}) collective-permute-start(bf16[16,144,128]{2,1,0:T(8,128)(2,1)S(1)} %get-tuple-element.54), channel_id=1, source_target_pairs={{0,2},{1,3},{2,16},{3,17},{4,6},{5,7},{6,20},{7,21},{8,10},{9,11},... | collective-permute-start | bytes 1769480 | tf_op jit(solution)/shard_map/ppermute | solution.py:53
  40.2 5.8 %collective-permute-start.5 = (bf16[16,144,128]{2,1,0:T(8,128)(2,1)S(1)}, bf16[16,144,128]{2,1,0:T(8,128)(2,1)S(1)}, u32[]{:S(2)}, u32[]{:S(2)}) collective-permute-start(bf16[16,144,128]{2,1,0:T(8,128)(2,1)S(1)} %get-tuple-element.55), channel_id=1, source_target_pairs={{2,0},{3,1},{6,4},{7,5},{10,8},{11,9},{14,12},{15,13},{16,2},{17,3... | collective-permute-start | bytes 1769480 | tf_op jit(solution)/shard_map/ppermute | solution.py:53
  46.1 6.6 %near_middle.1.refs_3_ = f32[32,32,128]{2,1,0:T(8,128)S(1)} custom-call(bf16[4,144,128]{2,1,0:T(8,128)(2,1)S(1)} %collective-permute-done.z_low.refs_0_, bf16[4,144,128]{2,1,0:T(8,128)(2,1)S(1)} %collective-permute-done.1.z_high.refs_1_, bf16[8,144,128]{2,1,0:T(8,128)(2,1)S(1)} %collective-permute-done.2.x_low.refs_2_, ...), custom_call_target="tpu_custom_call" | custom-call | flops 24999999488 | bytes 25000000 | tf_op jit(solution)/shard_map/near_middle/pallas_call | solution.py:501
  52.6 8.5 %widen.1.wide_hbm = bf16[7,2688,128]{2,1,0:T(8,128)(2,1)} custom-call(bf16[64,64,343]{2,1,0:T(8,128)(2,1)} %bitcast.48), custom_call_target="tpu_custom_call" | custom-call | flops 6000000000 | bytes 6000000 | tf_op jit(solution)/shard_map/widen/pallas_call | solution.py:558
  61.1 0.0 collective-permute-done.4.refs_0_
  61.1 0.0 collective-permute-done.5.refs_1_
  61.1 9.2 %near_last.1.near = f32[32,32,128]{2,1,0:T(8,128)S(1)} custom-call(bf16[16,144,128]{2,1,0:T(8,128)(2,1)S(1)} %collective-permute-done.4.refs_0_, bf16[16,144,128]{2,1,0:T(8,128)(2,1)S(1)} %collective-permute-done.5.refs_1_, bf16[32,128,48]{2,1,0:T(8,128)(2,1)S(1)} %get-tuple-element.44.refs_2_.refs_4_, f32[32,32,128]{2,1,0:T(8,128)S(1)} %near_middle.1.refs_3_, ...), custom_call_target="tpu_custom_call" | custom-call | flops 15000000512 | bytes 15000000 | tf_op jit(solution)/shard_map/near_last/pallas_call | solution.py:501
  70.3 0.0 copy-start.3
  70.3 0.8 copy-done.3
  71.1 24.5 %all-gather.3.cloned.1.call-done = bf16[4096,512]{1,0:T(8,128)(2,1)} async-done(((bf16[32,512]{1,0:T(8,128)(2,1)}), bf16[4096,512]{1,0:T(8,128)(2,1)}) %all-gather.3.cloned.1.call-update) | async-done | bytes 4194320 | tf_op jit(solution)/shard_map/all_gather | solution.py:539
  95.6 8.0 %far.1 = f32[8,32,512]{2,1,0:T(8,128)} custom-call(s32[8]{0:T(128)} %counts.3, bf16[64,2,32,512]{3,2,1,0:T(8,128)(2,1)} %bitcast.47, bf16[7,2688,128]{2,1,0:T(8,128)(2,1)} %widen.1.wide_hbm, bf16[8,64,64]{2,1,0:T(8,128)(2,1)} %up.1, bf16[8,64,64]{2,1,0:T(8,128)(2,1)} %down.1, bf16[8,64,512]{2,1,0:T(8,128)(2,1)} %get-tuple-element.57.shape, ...), custom_call_target="tpu_custom_call" | custom-call | flops 8000000000 | bytes 10000000 | tf_op jit(solution)/shard_map/far/pallas_call | solution.py:571
  (4 shorter events, 0.0 us)
Async XLA Ops:
  6.5 89.1 %all-gather.3.cloned.1.call-start = ((), (), s32[]{:S(2)}) async-start(), calls=%async_computation | async-start | bytes 4227072 | tf_op jit(solution)/shard_map/all_gather | solution.py:539
  6.5 7.9 %copy-start.2 = (s32[8]{0:T(128)S(1)}, s32[8]{0:T(128)}, u32[]{:S(2)}) copy-start(s32[8]{0:T(128)} %counts.3) | copy-start | bytes 100
  9.1 11.1 %collective-permute-start = (bf16[4,144,128]{2,1,0:T(8,128)(2,1)}, bf16[4,144,128]{2,1,0:T(8,128)(2,1)S(1)}, u32[]{:S(2)}, u32[]{:S(2)}) collective-permute-start(bf16[4,144,128]{2,1,0:T(8,128)(2,1)} %get-tuple-element.34.refs_1_), channel_id=1, source_target_pairs={{0,4},{1,5},{2,6},{3,7},{4,32},{5,33},{6,34},{7,35},{8,12},{9,13},... | collective-permute-start | bytes 442376 | tf_op jit(solution)/shard_map/ppermute | solution.py:53
  13.1 7.0 %collective-permute-start.1 = (bf16[4,144,128]{2,1,0:T(8,128)(2,1)}, bf16[4,144,128]{2,1,0:T(8,128)(2,1)S(1)}, u32[]{:S(2)}, u32[]{:S(2)}) collective-permute-start(bf16[4,144,128]{2,1,0:T(8,128)(2,1)} %get-tuple-element.35.refs_0_), channel_id=1, source_target_pairs={{4,0},{5,1},{6,2},{7,3},{12,8},{13,9},{14,10},{15,11},{20,16},{21,... | collective-permute-start | bytes 442376 | tf_op jit(solution)/shard_map/ppermute | solution.py:53
  14.4 0.9 copy-start
  15.3 0.9 copy-start.1
  20.3 8.4 %collective-permute-start.2 = (bf16[8,144,128]{2,1,0:T(8,128)(2,1)S(1)}, bf16[8,144,128]{2,1,0:T(8,128)(2,1)S(1)}, u32[]{:S(2)}, u32[]{:S(2)}) collective-permute-start(bf16[8,144,128]{2,1,0:T(8,128)(2,1)S(1)} %bitcast.46), channel_id=1, source_target_pairs={{0,1},{1,8},{2,3},{3,10},{4,5},{5,12},{6,7},{7,14},{8,9},{9,64},{1... | collective-permute-start | bytes 884744 | tf_op jit(solution)/shard_map/ppermute | solution.py:53
  23.4 14.2 %collective-permute-start.3 = (bf16[8,144,128]{2,1,0:T(8,128)(2,1)S(1)}, bf16[8,144,128]{2,1,0:T(8,128)(2,1)S(1)}, u32[]{:S(2)}, u32[]{:S(2)}) collective-permute-start(bf16[8,144,128]{2,1,0:T(8,128)(2,1)S(1)} %bitcast.45), channel_id=1, source_target_pairs={{1,0},{3,2},{5,4},{7,6},{8,1},{9,8},{10,3},{11,10},{12,5},{13,12},... | collective-permute-start | bytes 884744 | tf_op jit(solution)/shard_map/ppermute | solution.py:53
  37.7 23.4 %collective-permute-start.4 = (bf16[16,144,128]{2,1,0:T(8,128)(2,1)S(1)}, bf16[16,144,128]{2,1,0:T(8,128)(2,1)S(1)}, u32[]{:S(2)}, u32[]{:S(2)}) collective-permute-start(bf16[16,144,128]{2,1,0:T(8,128)(2,1)S(1)} %get-tuple-element.54), channel_id=1, source_target_pairs={{0,2},{1,3},{2,16},{3,17},{4,6},{5,7},{6,20},{7,21},{8,10},{9,11},... | collective-permute-start | bytes 1769480 | tf_op jit(solution)/shard_map/ppermute | solution.py:53
  40.2 20.9 %collective-permute-start.5 = (bf16[16,144,128]{2,1,0:T(8,128)(2,1)S(1)}, bf16[16,144,128]{2,1,0:T(8,128)(2,1)S(1)}, u32[]{:S(2)}, u32[]{:S(2)}) collective-permute-start(bf16[16,144,128]{2,1,0:T(8,128)(2,1)S(1)} %get-tuple-element.55), channel_id=1, source_target_pairs={{2,0},{3,1},{6,4},{7,5},{10,8},{11,9},{14,12},{15,13},{16,2},{17,3... | collective-permute-start | bytes 1769480 | tf_op jit(solution)/shard_map/ppermute | solution.py:53
  70.3 0.8 copy-start.3
Sparse Core Ops, SparseCore 0:
  10.5 85.0 all-gather.2
